TPU v7x, 32 devices: a whole 2x2x4 slice. The times are simulated.
32 devices in a mesh: rows: 8 (over z, y), cols: 4 (over x, core).
Axes of the slice: x: 2, y: 2, z: 4, core: 2. Of those that a mesh axis runs over, the one named last changes fastest.
Arguments:
- adjoint: float32 [3, 128, 384, 256], P(None, 'cols', 'rows'), may hold values from -6 to 6
- base_flow: bfloat16 [3, 128, 384, 256], P(None, 'cols', 'rows'), may hold values from -6 to 6
- stream_pair: bfloat16 [512, 256], replicated, may hold values from -0.375 to 0.375
- normal_pair: bfloat16 [768, 384], replicated, may hold values from -0.3125 to 0.3125
- span_pair: bfloat16 [256, 128], replicated, may hold values from -0.5 to 0.5
Outputs:
- adjoint_next: float32 [3, 128, 384, 256], P(None, 'cols', 'rows')
All inputs are finite; a program needn't handle non-finite values.
Results may differ from a plain program's by a relative error of at most 0.0023.
Values may be sent and summed in bfloat16 or wider, within the bound.
A program may use at most 128 MiB of HBM per device.

v0:
```python
import jax
import jax.numpy as jnp
from jax import lax
from jax.sharding import PartitionSpec as P

viscosity = 0.5
section_step = 0.5


def pack_lines(fields, pieces):
    count, outer, inner, length = fields.shape
    block = length // pieces
    split = fields.reshape(count, outer, inner, pieces, block)
    return split.transpose(0, 3, 1, 4, 2).reshape(count, pieces, outer, block * inner)


def unpack_lines(received, inner, outer_first):
    count, pieces, outer, merged = received.shape
    block = merged // inner
    split = received.reshape(count, pieces, outer, block, inner)
    if outer_first:
        return split.transpose(0, 2, 3, 1, 4).reshape(count, outer, block, pieces * inner)
    return split.transpose(0, 3, 2, 1, 4).reshape(count, block, outer, pieces * inner)


def direction_terms(lines, matrices, axis_index):
    length = lines.shape[3]
    adjoint_b = lines[:3]
    base_b = lines[3:]
    derivs = jnp.einsum("fabn,mn->fabm", adjoint_b, matrices, preferred_element_type=jnp.float32)
    first_deriv = derivs[..., :length]
    second = derivs[..., length:]
    base_deriv = jnp.einsum(
        "fabn,mn->fabm", base_b, matrices[:length], preferred_element_type=jnp.float32
    )
    adjoint_f = adjoint_b.astype(jnp.float32)
    base_f = base_b.astype(jnp.float32)
    transfer = jnp.sum(adjoint_f * base_deriv, axis=0)
    result = base_f[axis_index][None] * first_deriv + viscosity * second
    listing = [
        result[component] - transfer if component == axis_index else result[component]
        for component in range(3)
    ]
    return jnp.stack(listing)


def local(adjoint, base_flow, stream_pair, normal_pair, span_pair):
    row_count = lax.axis_size("rows")
    col_count = lax.axis_size("cols")
    stacked = jnp.concatenate([adjoint.astype(jnp.bfloat16), base_flow], axis=0)
    planes = stacked.shape[1]
    y_local = stacked.shape[2]
    terms_x = direction_terms(stacked, stream_pair, 0)

    def span_lines(portion):
        lines = unpack_lines(portion, planes, True)
        return direction_terms(lines, span_pair, 2)

    lines = unpack_lines(
        lax.all_to_all(
            pack_lines(stacked, row_count), "rows", split_axis=1, concat_axis=1, tiled=True
        ),
        y_local,
        False,
    )
    terms_y = direction_terms(lines, normal_pair, 1)
    terms_z = span_lines(
        lax.all_to_all(
            pack_lines(lines, col_count), "cols", split_axis=1, concat_axis=1, tiled=True
        )
    )
    returned = lax.all_to_all(
        pack_lines(terms_z, col_count), "cols", split_axis=1, concat_axis=1, tiled=True
    )
    gathered_y = terms_y + unpack_lines(returned, terms_z.shape[2], True)
    back = lax.all_to_all(
        pack_lines(gathered_y.transpose(0, 2, 1, 3), row_count),
        "rows",
        split_axis=1,
        concat_axis=1,
        tiled=True,
    )
    total = terms_x + unpack_lines(back, gathered_y.shape[1], True)
    return adjoint + section_step * total


def solution(mesh):
    placed = (P(None, "cols", "rows", None), P(None, "cols", "rows", None), P(), P(), P())
    return jax.shard_map(
        local, mesh=mesh, in_specs=placed, out_specs=P(None, "cols", "rows", None), check_vma=False
    )
```

profile of v0, /device:TPU:0, one launch (start us, length us, event | category | flops | bytes accessed | tf_op | source)
XLA Modules:
  0.0 758.8 jit_solution(8758813712117650248)
XLA Ops:
  0.0 2.8 convert_element_type.15
  6.7 20.9 %reshape.52 = bf16[6,32,48,8,32]{4,3,2,1,0:T(8,128)(2,1)} reshape(bf16[6,32,48,256]{3,2,1,0:T(8,128)(2,1)} %pad_maximum_fusion) | data formatting | bytes 9437184 | tf_op jit(solution)/shard_map/reshape | solution.py:13
  27.6 22.8 %copy.101 = bf16[6,8,32,32,48]{4,3,2,0,1:T(8,128)(2,1)} copy(bf16[6,8,32,32,48]{3,1,4,2,0:T(8,128)(2,1)} %bitcast.106) | data formatting | bytes 9437184 | tf_op jit(solution)/shard_map/reshape | solution.py:14
  50.4 23.7 %reshape.73 = bf16[6,8,32,1536]{3,2,0,1:T(8,128)(2,1)} reshape(bf16[6,8,32,32,48]{4,3,2,0,1:T(8,128)(2,1)} %copy.101) | data formatting | bytes 9437184 | tf_op jit(solution)/shard_map/reshape | solution.py:14
  74.1 111.7 %all_to_all.20 = bf16[6,8,32,1536]{3,2,0,1:T(8,128)(2,1)S(1)} all-to-all(bf16[6,8,32,1536]{3,2,0,1:T(8,128)(2,1)} %reshape.73), channel_id=1, replica_groups=mesh['rows'=8,'cols'=4] {'rows'}, dimensions={1} | all-to-all | bytes 9437184 | tf_op jit(solution)/shard_map/all_to_all | solution.py:60
  188.3 17.1 %reshape.54 = bf16[6,8,32,32,48]{4,3,2,1,0:T(8,128)(2,1)} reshape(bf16[6,8,32,1536]{3,2,1,0:T(8,128)(2,1)} %copy.70) | data formatting | bytes 9437184 | tf_op jit(solution)/shard_map/reshape | solution.py:20
  205.5 14.4 %copy.74 = bf16[6,32,32,8,48]{4,3,2,1,0:T(8,128)(2,1)} copy(bf16[6,32,32,8,48]{4,1,2,3,0:T(8,128)(2,1)} %bitcast.102) | data formatting | bytes 9437184 | tf_op jit(solution)/shard_map/transpose | solution.py:23
  219.9 17.3 %reshape_reshape.3 = bf16[6,32,32,4,96]{4,3,2,1,0:T(4,128)(2,1)} reshape(bf16[6,32,32,8,48]{4,3,2,1,0:T(8,128)(2,1)} %copy.74) | data formatting | bytes 9437184 | tf_op jit(solution)/shard_map/reshape;reshape | solution.py:13
  237.2 19.0 %copy.102 = bf16[6,4,32,96,32]{4,3,2,0,1:T(8,128)(2,1)} copy(bf16[6,4,32,96,32]{3,1,4,2,0:T(4,128)(2,1)} %bitcast.113) | data formatting | bytes 9437184 | tf_op jit(solution)/shard_map/reshape | solution.py:14
  256.2 24.5 %reshape.74 = bf16[6,4,32,3072]{3,2,0,1:T(8,128)(2,1)} reshape(bf16[6,4,32,96,32]{4,3,2,0,1:T(8,128)(2,1)} %copy.102) | data formatting | bytes 9437184 | tf_op jit(solution)/shard_map/reshape | solution.py:14
  280.8 60.0 %all_to_all.21 = bf16[6,4,32,3072]{3,2,0,1:T(8,128)(2,1)} all-to-all(bf16[6,4,32,3072]{3,2,0,1:T(8,128)(2,1)} %reshape.74), channel_id=1, replica_groups=mesh['rows'=8,'cols'=4] {'cols'}, dimensions={1} | all-to-all | bytes 9437184 | tf_op jit(solution)/shard_map/all_to_all | solution.py:68
  340.8 21.3 %reshape.75 = bf16[6,4,32,96,32]{4,3,2,0,1:T(8,128)(2,1)} reshape(bf16[6,4,32,3072]{3,2,0,1:T(8,128)(2,1)} %all_to_all.21) | data formatting | bytes 9437184 | tf_op jit(solution)/shard_map/reshape | solution.py:20
  362.0 16.1 %copy.78 = bf16[6,4,32,96,32]{3,4,1,2,0:T(8,128)(2,1)} copy(bf16[6,4,32,96,32]{4,3,2,0,1:T(8,128)(2,1)} %reshape.75) | data formatting | bytes 9437184 | tf_op jit(solution)/shard_map/reshape | solution.py:20
  378.2 6.5 fusion.19
  389.7 5.1 fusion.14
  396.2 5.0 fusion
  401.3 3.6 copy-done.6
  408.1 3.0 copy.84
  411.1 3.3 copy.81
  414.3 6.9 maximum_bitcast_fusion
  421.2 8.3 %reshape.76 = f32[3,4,32,3072]{3,1,2,0:T(4,128)} reshape(f32[3,4,32,32,96]{4,3,1,2,0:T(8,128)} %maximum_bitcast_fusion) | data formatting | bytes 9437184 | tf_op jit(solution)/shard_map/reshape | solution.py:14
  429.5 7.2 copy.86
  436.7 5.4 all-to-all-start.2
  442.2 9.3 %fusion.18 = (bf16[3,32,32,8,48]{4,1,2,3,0:T(8,128)(2,1)}, bf16[3,32,32,8,48]{4,1,2,3,0:T(8,128)(2,1)S(1)}) fusion(bf16[6,32,32,8,48]{4,1,2,3,0:T(8,128)(2,1)} %bitcast.103), kind=kLoop, calls=%fused_computation.36 | loop fusion | bytes 9437184 | tf_op jit(solution)/shard_map/slice | solution.py:29
  451.4 6.7 copy.72
  458.1 8.1 %slice.100 = bf16[3,32,32,384]{3,2,1,0:T(8,128)(2,1)S(1)} reshape(bf16[3,32,32,8,48]{4,3,2,1,0:T(8,128)(2,1)} %copy.72) | data formatting | bytes 4718592 | tf_op jit(solution)/shard_map/slice | solution.py:28
  466.2 9.5 %copy.73 = bf16[3,32,32,8,48]{4,3,2,1,0:T(8,128)(2,1)} copy(bf16[3,32,32,8,48]{4,1,2,3,0:T(8,128)(2,1)} %get-tuple-element.5) | data formatting | bytes 4718592 | tf_op jit(solution)/shard_map/slice | solution.py:29
  475.7 9.3 %slice.106 = bf16[3,32,32,384]{3,2,1,0:T(8,128)(2,1)} reshape(bf16[3,32,32,8,48]{4,3,2,1,0:T(8,128)(2,1)} %copy.73) | data formatting | bytes 4718592 | tf_op jit(solution)/shard_map/slice | solution.py:29
  487.1 4.4 copy.71
  491.6 4.6 reshape.65
  496.2 3.8 multiply_reduce_fusion.1
  505.2 5.1 copy.87
  510.3 7.5 reshape.58
  517.8 11.5 %copy.88 = f32[3,32,32,4,96]{4,3,2,1,0:T(4,128)} copy(f32[3,32,32,4,96]{4,2,1,3,0:T(8,128)} %bitcast.112) | data formatting | bytes 9437184 | tf_op jit(solution)/shard_map/transpose | solution.py:22
  529.3 7.6 %reshape.59 = f32[3,32,32,384]{3,2,1,0:T(8,128)} reshape(f32[3,32,32,4,96]{4,3,2,1,0:T(4,128)} %copy.88) | data formatting | bytes 9437184 | tf_op jit(solution)/shard_map/reshape | solution.py:22
  537.0 6.1 fusion.5
  543.0 10.3 %reshape.60 = f32[3,32,32,8,48]{4,3,1,2,0:T(8,128)} reshape(f32[3,32,32,384]{3,1,2,0:T(8,128)} %fusion.5) | data formatting | bytes 9437184 | tf_op jit(solution)/shard_map/reshape | solution.py:13
  553.4 16.4 %copy.89 = f32[3,32,32,8,48]{2,4,1,3,0:T(8,128)} copy(f32[3,32,32,8,48]{4,3,1,2,0:T(8,128)} %reshape.60) | data formatting | bytes 9437184 | tf_op jit(solution)/shard_map/reshape | solution.py:13
  569.8 14.3 %reshape.61 = f32[3,8,32,1536]{3,2,1,0:T(8,128)} reshape(f32[3,8,32,48,32]{4,3,2,1,0:T(8,128)} %bitcast.107) | data formatting | bytes 9437184 | tf_op jit(solution)/shard_map/reshape | solution.py:14
  584.1 5.1 copy.90
  589.1 5.1 all-to-all-start.3
  598.0 3.4 copy-done.3
  603.8 95.7 %all-to-all-done.3 = f32[3,8,32,1536]{3,2,0,1:T(8,128)} async-done(((f32[3,8,32,1536]{3,2,0,1:T(8,128)}), f32[3,8,32,1536]{3,2,0,1:T(8,128)}, u32[]{:S(2)}, u32[]{:S(2)}) %all-to-all-start.3) | async-done | bytes 4718624 | tf_op jit(solution)/shard_map/all_to_all | solution.py:76
  699.6 5.1 copy.91
  704.6 12.2 %reshape.62 = f32[3,8,32,48,32]{4,3,2,1,0:T(8,128)} reshape(f32[3,8,32,1536]{3,2,1,0:T(8,128)} %copy.91) | data formatting | bytes 9437184 | tf_op jit(solution)/shard_map/reshape | solution.py:20
  716.8 19.6 %copy.92 = f32[3,32,48,8,32]{4,3,2,1,0:T(8,128)} copy(f32[3,32,48,8,32]{4,2,1,3,0:T(8,128)} %bitcast.105) | data formatting | bytes 9437184 | tf_op jit(solution)/shard_map/transpose | solution.py:22
  736.4 14.0 %reshape.63 = f32[3,32,48,256]{3,2,1,0:T(8,128)} reshape(f32[3,32,48,8,32]{4,3,2,1,0:T(8,128)} %copy.92) | data formatting | bytes 9437184 | tf_op jit(solution)/shard_map/reshape | solution.py:22
  750.4 8.0 %fusion.4 = f32[3,32,48,256]{3,2,1,0:T(8,128)} fusion(f32[3,32,48,256]{3,2,1,0:T(8,128)} %param.5, f32[3,32,48,256]{3,2,1,0:T(8,128)} %reshape.63, f32[2,32,48,256]{3,2,1,0:T(8,128)S(1)} %slice-done.1, f32[1,32,48,256]{3,2,1,0:T(8,128)} %slice_subtract_fusion.2), kind=kLoop, calls=%fused_computation.12 | loop fusion | flops 4718592 | bytes 18874368 | tf_op jit(solution)/shard_map/add | solution.py:84
  (43 shorter events, 29.6 us)
Async XLA Ops:
  0.0 4.1 copy-start.2
  2.8 1.4 copy-start
  384.7 5.0 copy-start.11
  401.3 5.4 copy-start.4
  401.3 3.6 copy-start.6
  401.3 4.3 copy-start.7
  408.1 3.0 slice-start
  436.7 68.5 %all-to-all-start.2 = ((f32[3,4,32,3072]{3,2,0,1:T(8,128)}), f32[3,4,32,3072]{3,2,0,1:T(8,128)}, u32[]{:S(2)}, u32[]{:S(2)}) async-start(f32[3,4,32,3072]{3,2,0,1:T(8,128)} %copy.86), calls=%async_computation.2 | async-start | bytes 9437184 | tf_op jit(solution)/shard_map/all_to_all | solution.py:72
  491.6 4.6 copy-start.10
  500.0 2.7 copy-start.8
  589.1 6.5 copy-start.1
  589.1 6.5 copy-start.9
  589.1 110.4 %all-to-all-start.3 = ((f32[3,8,32,1536]{3,2,0,1:T(8,128)}), f32[3,8,32,1536]{3,2,0,1:T(8,128)}, u32[]{:S(2)}, u32[]{:S(2)}) async-start(f32[3,8,32,1536]{3,2,0,1:T(8,128)} %copy.90), calls=%async_computation.3 | async-start | bytes 9437184 | tf_op jit(solution)/shard_map/all_to_all | solution.py:76
  598.0 4.4 copy-start.5
  598.0 3.4 copy-start.3
  736.4 14.0 %slice-start.1 = ((f32[3,32,48,256]{3,2,1,0:T(8,128)}), f32[2,32,48,256]{3,2,1,0:T(8,128)S(1)}, s32[]{:S(2)}) async-start(f32[3,32,48,256]{3,2,1,0:T(8,128)} %copy-done.5), calls=%async_computation.5 | async-start | bytes 6291456 | tf_op jit(solution)/shard_map/slice | solution.py:41
where the time goes:
time: 772 us; the launch traced here: 759 us
  local copies, waits for them, and re-layouts  424 us (55%)
  blocking collectives  172 us (22%)
  waiting for transfers between devices  95.7 us (12%)
  other arithmetic  41.1 us (5%)
  matrix products  15 us (2%)
  starting transfers between devices  10.5 us (1%)
    reshape x8, local copies, waits for them, and re-layouts, pack_lines(): split.transpose(0, 3, 1, 4, 2).reshape(count, pieces, outer, block * inner)  125 us
    all_to_all x1, blocking collectives, local(): lax.all_to_all(pack_lines(stacked, row_count), 'rows', split_axis=1, conc...  112 us
    all_to_all x1, waiting for transfers between devices, local(): lax.all_to_all(pack_lines(gathered_y.transpose(0, 2, 1, 3), row_count), '...  95.7 us
    reshape x5, local copies, waits for them, and re-layouts, unpack_lines(): split = received.reshape(count, pieces, outer, block, inner)  74.3 us
    all_to_all x1, blocking collectives, local(): lax.all_to_all(pack_lines(lines, col_count), 'cols', split_axis=1, concat...  60 us
    reshape x3, local copies, waits for them, and re-layouts, pack_lines(): split = fields.reshape(count, outer, inner, pieces, block)  47.6 us
    slice x4, local copies, waits for them, and re-layouts, direction_terms(): base_b = lines[3:]  34.5 us
    transpose x2, local copies, waits for them, and re-layouts, unpack_lines(): split.transpose(0, 2, 3, 1, 4).reshape(count, outer, block, pieces * inner)  31.1 us
  transfers between devices with their start and end apart: 2, of which 1 were waited for; matrix products, arithmetic and copies ran while one was open for 9% of the time, Pallas kernels for 0%

commit v1 on v0

--- a/solution.py
+++ b/solution.py
@@ -1,6 +1,10 @@
+import functools
+
 import jax
 import jax.numpy as jnp
 from jax import lax
+from jax.experimental import pallas as pl
+from jax.experimental.pallas import tpu as pltpu
 from jax.sharding import PartitionSpec as P
 
 viscosity = 0.5
@@ -84,8 +88,290 @@
     return adjoint + section_step * total
 
 
+def section_kernel(
+    rows, cols, adjoint, base, stream_t, normal, span, out,
+    a_bf, y_a, y_u, z_src, z_recv, y_term, y_back, z_term, z_back,
+    ya_send, ya_recv, yu_send, yu_recv, yb_send, yb_recv, z_send, z_recv_sem, zb_send, zb_recv,
+):
+    row = lax.axis_index("rows")
+    col = lax.axis_index("cols")
+    _, nz, ny, nx = adjoint.shape
+    zc = nz // rows
+    yc = ny // cols
+
+    def row_at(offset):
+        return lax.rem(row + offset, rows)
+
+    def col_at(offset):
+        return lax.rem(col + offset, cols)
+
+    barrier = pltpu.get_barrier_semaphore()
+    for offset in range(1, rows):
+        pl.semaphore_signal(
+            barrier, inc=1, device_id={"rows": row_at(offset)}, device_id_type=pl.DeviceIdType.MESH
+        )
+    for offset in range(1, cols):
+        pl.semaphore_signal(
+            barrier, inc=1, device_id={"cols": col_at(offset)}, device_id_type=pl.DeviceIdType.MESH
+        )
+    pl.semaphore_wait(barrier, rows + cols - 2)
+
+    def to_row(src, dst, send, recv, peer, chunk, source):
+        return pltpu.make_async_remote_copy(
+            src_ref=src, dst_ref=dst, send_sem=send.at[chunk, peer], recv_sem=recv.at[chunk, source],
+            device_id={"rows": peer}, device_id_type=pl.DeviceIdType.MESH,
+        )
+
+    def to_col(src, dst, send, recv, peer, source):
+        return pltpu.make_async_remote_copy(
+            src_ref=src, dst_ref=dst, send_sem=send.at[peer], recv_sem=recv.at[source],
+            device_id={"cols": peer}, device_id_type=pl.DeviceIdType.MESH,
+        )
+
+    def y_rows(index):
+        return pl.ds(pl.multiple_of(index * ny, 16), ny)
+
+    def z_rows(index):
+        return pl.ds(pl.multiple_of(index * nz, 16), nz)
+
+    def fwd_a(peer, chunk, source):
+        return to_row(
+            a_bf.at[:, peer * zc + chunk], y_a.at[:, chunk, y_rows(source)],
+            ya_send, ya_recv, peer, chunk, source,
+        )
+
+    def fwd_u(peer, chunk, source):
+        return to_row(
+            base.at[:, peer * zc + chunk], y_u.at[:, chunk, y_rows(source)],
+            yu_send, yu_recv, peer, chunk, source,
+        )
+
+    def back_y(peer, chunk, source):
+        return to_row(
+            y_term.at[:, chunk, y_rows(peer)], y_back.at[:, source * zc + chunk],
+            yb_send, yb_recv, peer, chunk, source,
+        )
+
+    def fwd_z(peer, source):
+        return to_col(
+            z_src.at[:, pl.ds(peer * yc, yc)], z_recv.at[:, :, z_rows(source)],
+            z_send, z_recv_sem, peer, source,
+        )
+
+    def back_z(peer, source):
+        return to_col(
+            z_term.at[:, :, z_rows(peer)], z_back.at[:, pl.ds(source * yc, yc)],
+            zb_send, zb_recv, peer, source,
+        )
+
+    def row_loop(body):
+        @pl.loop(1, rows)
+        def _(offset):
+            body(row_at(offset))
+
+    def col_loop(body):
+        @pl.loop(1, cols)
+        def _(offset):
+            body(col_at(offset))
+
+    @pl.loop(0, nz)
+    def _(z):
+        a_bf[:, z] = adjoint[:, z].astype(jnp.bfloat16)
+
+    @pl.loop(0, zc)
+    def _(chunk):
+        @pl.loop(1, rows)
+        def _(offset):
+            peer = row_at(offset)
+            fwd_a(peer, chunk, row).start()
+            fwd_u(peer, chunk, row).start()
+
+    @pl.loop(0, 3)
+    def _(field):
+        for z0 in range(0, nz, 16):
+            z_src[field, :, z0 : z0 + 16, :] = jnp.swapaxes(
+                adjoint[field, z0 : z0 + 16], 0, 1
+            ).astype(jnp.bfloat16)
+            z_src[3 + field, :, z0 : z0 + 16, :] = jnp.swapaxes(
+                base[field, z0 : z0 + 16].astype(jnp.float32), 0, 1
+            ).astype(jnp.bfloat16)
+
+    col_loop(lambda peer: fwd_z(peer, col).start())
+
+    def terms(adj, flow, own, derive, length, axis):
+        half = flow[own].astype(jnp.float32)
+        transfer = None
+        for field in range(3):
+            part = adj[field].astype(jnp.float32) * derive(flow[field], False)
+            transfer = part if transfer is None else transfer + part
+        listing = []
+        for field in range(3):
+            both = derive(adj[field], True)
+            first = lax.slice_in_dim(both, 0, length, axis=axis)
+            second = lax.slice_in_dim(both, length, 2 * length, axis=axis)
+            term = half * first + viscosity * second
+            listing.append(term - transfer if field == own else term)
+        return listing
+
+    step = 4
+    @pl.loop(0, nz // step)
+    def _(part):
+        planes = pl.ds(part * step, step)
+
+        def derive(lines, both):
+            matrix = stream_t[...] if both else stream_t[:, :nx]
+            return jnp.dot(lines, matrix, preferred_element_type=jnp.float32)
+
+        adj = [a_bf[field, planes].reshape(step * ny, nx) for field in range(3)]
+        flow = [base[field, planes].reshape(step * ny, nx) for field in range(3)]
+        for field, term in enumerate(terms(adj, flow, 0, derive, nx, 1)):
+            out[field, planes] = adjoint[field, planes] + section_step * term.reshape(step, ny, nx)
+
+    def column_terms(matrix_ref, adj, flow, own):
+        length = matrix_ref.shape[1]
+
+        def derive(lines, both):
+            matrix = matrix_ref[...] if both else matrix_ref[:length]
+            return jnp.dot(matrix, lines, preferred_element_type=jnp.float32)
+
+        return terms(adj, flow, own, derive, length, 0)
+
+    @pl.loop(0, zc)
+    def _(chunk):
+        for field in range(3):
+            y_a[field, chunk, y_rows(row), :] = a_bf[field, row * zc + chunk]
+            y_u[field, chunk, y_rows(row), :] = base[field, row * zc + chunk]
+
+    @pl.loop(0, yc)
+    def _(line):
+        for field in range(6):
+            z_recv[field, line, z_rows(col), :] = z_src[field, col * yc + line]
+
+    def y_chunk(chunk):
+        @pl.loop(1, rows)
+        def _(offset):
+            source = row_at(offset)
+            fwd_a(source, chunk, source).wait_recv()
+            fwd_u(source, chunk, source).wait_recv()
+
+        adj = [y_a[field, chunk] for field in range(3)]
+        flow = [y_u[field, chunk] for field in range(3)]
+        for field, term in enumerate(column_terms(normal, adj, flow, 1)):
+            y_term[field, chunk] = term.astype(jnp.bfloat16)
+
+        @pl.loop(1, rows)
+        def _(offset):
+            back_y(row_at(offset), chunk, row).start()
+
+        for field in range(3):
+            out[field, row * zc + chunk] += section_step * y_term[
+                field, chunk, y_rows(row), :
+            ].astype(jnp.float32)
+
+    early = zc // 2
+
+    @pl.loop(0, early)
+    def _(chunk):
+        y_chunk(chunk)
+
+    col_loop(lambda source: fwd_z(source, source).wait_recv())
+
+    @pl.loop(0, yc)
+    def _(line):
+        adj = [z_recv[field, line] for field in range(3)]
+        flow = [z_recv[3 + field, line] for field in range(3)]
+        for field, term in enumerate(column_terms(span, adj, flow, 2)):
+            z_term[field, line] = term.astype(jnp.bfloat16)
+
+    col_loop(lambda peer: back_z(peer, col).start())
+
+    @pl.loop(0, yc)
+    def _(line):
+        for field in range(3):
+            z_back[field, col * yc + line] = z_term[field, line, z_rows(col), :]
+
+    @pl.loop(early, zc)
+    def _(chunk):
+        y_chunk(chunk)
+
+    col_loop(lambda source: back_z(source, source).wait_recv())
+
+    @pl.loop(0, 3)
+    def _(field):
+        for z0 in range(0, nz, 16):
+            out[field, z0 : z0 + 16] += section_step * jnp.swapaxes(
+                z_back[field, :, z0 : z0 + 16, :].astype(jnp.float32), 0, 1
+            )
+
+    @pl.loop(0, zc)
+    def _(chunk):
+        @pl.loop(1, rows)
+        def _(offset):
+            source = row_at(offset)
+            back_y(source, chunk, source).wait_recv()
+            plane = source * zc + chunk
+            out[:, plane] += section_step * y_back[:, plane].astype(jnp.float32)
+
+    @pl.loop(0, zc)
+    def _(chunk):
+        @pl.loop(1, rows)
+        def _(offset):
+            peer = row_at(offset)
+            fwd_a(peer, chunk, row).wait_send()
+            fwd_u(peer, chunk, row).wait_send()
+            back_y(peer, chunk, row).wait_send()
+
+    @pl.loop(1, cols)
+    def _(offset):
+        peer = col_at(offset)
+        fwd_z(peer, col).wait_send()
+        back_z(peer, col).wait_send()
+
+
+def local_kernel(adjoint, base_flow, stream_pair, normal_pair, span_pair):
+    rows = lax.axis_size("rows")
+    cols = lax.axis_size("cols")
+    _, nz, ny, nx = adjoint.shape
+    zc, yc = nz // rows, ny // cols
+    bf = jnp.bfloat16
+    vmem = pl.BlockSpec(memory_space=pltpu.VMEM)
+    row_sems = [pltpu.SemaphoreType.DMA((zc, rows))] * 6
+    col_sems = [pltpu.SemaphoreType.DMA((cols,))] * 4
+    return pl.pallas_call(
+        functools.partial(section_kernel, rows, cols),
+        out_shape=jax.ShapeDtypeStruct(adjoint.shape, jnp.float32),
+        in_specs=[vmem] * 5,
+        out_specs=vmem,
+        scratch_shapes=[
+            pltpu.VMEM((3, nz, ny, nx), bf),
+            pltpu.VMEM((3, zc, rows * ny, nx), bf),
+            pltpu.VMEM((3, zc, rows * ny, nx), bf),
+            pltpu.VMEM((6, ny, nz, nx), bf),
+            pltpu.VMEM((6, yc, cols * nz, nx), bf),
+            pltpu.VMEM((3, zc, rows * ny, nx), bf),
+            pltpu.VMEM((3, nz, ny, nx), bf),
+            pltpu.VMEM((3, yc, cols * nz, nx), bf),
+            pltpu.VMEM((3, ny, nz, nx), bf),
+            *row_sems,
+            *col_sems,
+        ],
+        compiler_params=pltpu.CompilerParams(
+            collective_id=0, has_side_effects=True, vmem_limit_bytes=60 * 1024 * 1024
+        ),
+    )(adjoint, base_flow, stream_pair.T, normal_pair, span_pair)
+
+
+def section(adjoint, base_flow, stream_pair, normal_pair, span_pair):
+    _, nz, ny, nx = adjoint.shape
+    rows, cols = lax.axis_size("rows"), lax.axis_size("cols")
+    whole = nz % 16 == 0 and ny % 16 == 0 and nx % 128 == 0
+    if whole and nz % rows == 0 and ny % cols == 0:
+        return local_kernel(adjoint, base_flow, stream_pair, normal_pair, span_pair)
+    return local(adjoint, base_flow, stream_pair, normal_pair, span_pair)
+
+
 def solution(mesh):
     placed = (P(None, "cols", "rows", None), P(None, "cols", "rows", None), P(), P(), P())
     return jax.shard_map(
-        local, mesh=mesh, in_specs=placed, out_specs=P(None, "cols", "rows", None), check_vma=False
-    )
+        section, mesh=mesh, in_specs=placed, out_specs=P(None, "cols", "rows", None), check_vma=False
+    )

time: 772 us -> 173 us (0.22); the launches traced: 759 us -> 170 us
  local copies, waits for them, and re-layouts: 424 us -> 6.66 us
  blocking collectives: 172 us -> 0 us
  Pallas kernels: 0 us -> 164 us
  waiting for transfers between devices: 95.7 us -> 0 us
  other arithmetic: 41.1 us -> 0 us
  matrix products: 15 us -> 0 us
  starting transfers between devices: 10.5 us -> 0 us
    reshape x18 -> x0, local copies, waits for them, and re-layouts: 268 us -> none  [the longest x8 125 us: pack_lines(): split.transpose(0, 3, 1, 4, 2).reshape(count, pieces, outer, block * inner)]
    all_to_all x2 -> x0, blocking collectives: 172 us -> none  [the longest x1 112 us: local(): lax.all_to_all(pack_lines(stacked, row_count), 'rows', split_axis=1, conc...]
    pallas_call x0 -> x1, Pallas kernels: none -> 164 us  [local_kernel(): pl.pallas_call(functools.partial(section_kernel, rows, cols), out_shape=j...]
    all_to_all x2 -> x0, waiting for transfers between devices: 95.7 us -> none  [the longest x1 95.7 us: local(): lax.all_to_all(pack_lines(gathered_y.transpose(0, 2, 1, 3), row_count), '...]
    slice x13 -> x0, local copies, waits for them, and re-layouts: 57.6 us -> none  [the longest x4 34.5 us: direction_terms(): base_b = lines[3:]]
    transpose x3 -> x0, local copies, waits for them, and re-layouts: 45.6 us -> none  [the longest x2 31.1 us: unpack_lines(): split.transpose(0, 2, 3, 1, 4).reshape(count, outer, block, pieces * inner)]
    another operation x1 -> x0, local copies, waits for them, and re-layouts: 17.3 us -> none  [pack_lines(): split = fields.reshape(count, outer, inner, pieces, block)]
    dot_general x6 -> x0, matrix products: 15 us -> none  [the longest x3 9.15 us: direction_terms(): jnp.einsum('fabn,mn->fabm', adjoint_b, matrices, preferred_element_type=j...]
  transfers between devices with their start and end apart: 2 -> 0, of which waited for: 1 -> 0; matrix products, arithmetic and copies ran while one was open for 9% -> 0% of each run, Pallas kernels for 0% -> 0%
where the time goes in v1:
time: 173 us; the launch traced here: 170 us
  Pallas kernels  164 us (95%)
  local copies, waits for them, and re-layouts  6.66 us (4%)
    pallas_call x1, Pallas kernels, local_kernel(): pl.pallas_call(functools.partial(section_kernel, rows, cols), out_shape=j...  164 us
    unnamed x2, local copies, waits for them, and re-layouts  6.66 us

profile of v1, /device:TPU:0, one launch (start us, length us, event | category | flops | bytes accessed | tf_op | source)
XLA Modules:
  0.0 170.3 jit_solution(17559918490974572184)
XLA Ops:
  0.0 1.8 %copy.6 = bf16[512,256]{0,1:T(8,128)(2,1)} copy(bf16[512,256]{1,0:T(8,128)(2,1)} %param.7) | data formatting | bytes 524288 | tf_op args[2]
  1.8 163.7 %shard_map.55 = f32[3,32,48,256]{3,2,1,0:T(8,128)} custom-call(f32[3,32,48,256]{3,2,1,0:T(8,128)} %adjoint.1, bf16[3,32,48,256]{3,2,1,0:T(8,128)(2,1)} %base.1, bf16[256,512]{1,0:T(8,128)(2,1)} %bitcast.1, bf16[768,384]{1,0:T(8,128)(2,1)} %normal.1, bf16[256,128]{1,0:T(8,128)(2,1)} %span.1), custom_call_target="tpu_custom_call" | custom-call | tf_op jit(solution)/shard_map/pallas_call | solution.py:340
  165.5 4.9 %copy.8 = f32[3,32,48,256]{3,2,1,0:T(8,128)} copy(f32[3,32,48,256]{3,2,1,0:T(8,128)} %shard_map.55) | data formatting | bytes 9437184

commit v2 on v1

--- a/solution.py
+++ b/solution.py
@@ -89,15 +89,23 @@
 
 
 def section_kernel(
-    rows, cols, adjoint, base, stream_t, normal, span, out,
-    a_bf, y_a, y_u, z_src, z_recv, y_term, y_back, z_term, z_back,
+    rows, cols, adjoint_hbm, base_hbm, stream, normal, span, out_hbm, y_back,
+    out, base, a_bf, y_a, y_u, z_src, z_recv, y_term, z_term, z_back,
     ya_send, ya_recv, yu_send, yu_recv, yb_send, yb_recv, z_send, z_recv_sem, zb_send, zb_recv,
+    own_sem, load_sem,
 ):
     row = lax.axis_index("rows")
     col = lax.axis_index("cols")
-    _, nz, ny, nx = adjoint.shape
+    _, nz, ny, nx = out.shape
     zc = nz // rows
     yc = ny // cols
+    half_rows = rows // 2
+    own_half = row // half_rows
+
+    load_adjoint = pltpu.make_async_copy(adjoint_hbm, out, load_sem.at[0])
+    load_base = pltpu.make_async_copy(base_hbm, base, load_sem.at[1])
+    load_adjoint.start()
+    load_base.start()
 
     def row_at(offset):
         return lax.rem(row + offset, rows)
@@ -142,7 +150,7 @@
 
     def fwd_u(peer, chunk, source):
         return to_row(
-            base.at[:, peer * zc + chunk], y_u.at[:, chunk, y_rows(source)],
+            base_hbm.at[:, peer * zc + chunk], y_u.at[:, chunk, y_rows(source)],
             yu_send, yu_recv, peer, chunk, source,
         )
 
@@ -152,6 +160,11 @@
             yb_send, yb_recv, peer, chunk, source,
         )
 
+    def own_y(chunk):
+        return pltpu.make_async_copy(
+            y_term.at[:, chunk, y_rows(row)], y_back.at[:, row * zc + chunk], own_sem.at[chunk]
+        )
+
     def fwd_z(peer, source):
         return to_col(
             z_src.at[:, pl.ds(peer * yc, yc)], z_recv.at[:, :, z_rows(source)],
@@ -165,32 +178,43 @@
         )
 
     def row_loop(body):
-        @pl.loop(1, rows)
-        def _(offset):
-            body(row_at(offset))
+        @pl.loop(0, half_rows)
+        def _(offset):
+            body((1 - own_half) * half_rows + lax.rem(row + offset, half_rows))
+
+        @pl.loop(1, half_rows)
+        def _(offset):
+            body(own_half * half_rows + lax.rem(row + offset, half_rows))
 
     def col_loop(body):
         @pl.loop(1, cols)
         def _(offset):
             body(col_at(offset))
 
+    row_loop(lambda peer: fwd_u(peer, 0, row).start())
+    load_adjoint.wait()
+
     @pl.loop(0, nz)
     def _(z):
-        a_bf[:, z] = adjoint[:, z].astype(jnp.bfloat16)
-
-    @pl.loop(0, zc)
-    def _(chunk):
-        @pl.loop(1, rows)
-        def _(offset):
-            peer = row_at(offset)
+        a_bf[:, z] = out[:, z].astype(jnp.bfloat16)
+
+    row_loop(lambda peer: fwd_a(peer, 0, row).start())
+
+    @pl.loop(1, zc)
+    def _(chunk):
+        def both(peer):
             fwd_a(peer, chunk, row).start()
             fwd_u(peer, chunk, row).start()
+
+        row_loop(both)
+
+    load_base.wait()
 
     @pl.loop(0, 3)
     def _(field):
         for z0 in range(0, nz, 16):
             z_src[field, :, z0 : z0 + 16, :] = jnp.swapaxes(
-                adjoint[field, z0 : z0 + 16], 0, 1
+                out[field, z0 : z0 + 16], 0, 1
             ).astype(jnp.bfloat16)
             z_src[3 + field, :, z0 : z0 + 16, :] = jnp.swapaxes(
                 base[field, z0 : z0 + 16].astype(jnp.float32), 0, 1
@@ -219,13 +243,15 @@
         planes = pl.ds(part * step, step)
 
         def derive(lines, both):
-            matrix = stream_t[...] if both else stream_t[:, :nx]
-            return jnp.dot(lines, matrix, preferred_element_type=jnp.float32)
+            matrix = stream[...] if both else stream[:nx]
+            return lax.dot_general(
+                lines, matrix, (((1,), (1,)), ((), ())), preferred_element_type=jnp.float32
+            )
 
         adj = [a_bf[field, planes].reshape(step * ny, nx) for field in range(3)]
         flow = [base[field, planes].reshape(step * ny, nx) for field in range(3)]
         for field, term in enumerate(terms(adj, flow, 0, derive, nx, 1)):
-            out[field, planes] = adjoint[field, planes] + section_step * term.reshape(step, ny, nx)
+            out[field, planes] += section_step * term.reshape(step, ny, nx)
 
     def column_terms(matrix_ref, adj, flow, own):
         length = matrix_ref.shape[1]
@@ -259,14 +285,8 @@
         for field, term in enumerate(column_terms(normal, adj, flow, 1)):
             y_term[field, chunk] = term.astype(jnp.bfloat16)
 
-        @pl.loop(1, rows)
-        def _(offset):
-            back_y(row_at(offset), chunk, row).start()
-
-        for field in range(3):
-            out[field, row * zc + chunk] += section_step * y_term[
-                field, chunk, y_rows(row), :
-            ].astype(jnp.float32)
+        row_loop(lambda peer: back_y(peer, chunk, row).start())
+        own_y(chunk).start()
 
     early = zc // 2
 
@@ -303,14 +323,19 @@
                 z_back[field, :, z0 : z0 + 16, :].astype(jnp.float32), 0, 1
             )
 
+    store = pltpu.make_async_copy(out, out_hbm, load_sem.at[0])
+    store.start()
+
     @pl.loop(0, zc)
     def _(chunk):
+        own_y(chunk).wait()
+
         @pl.loop(1, rows)
         def _(offset):
             source = row_at(offset)
             back_y(source, chunk, source).wait_recv()
-            plane = source * zc + chunk
-            out[:, plane] += section_step * y_back[:, plane].astype(jnp.float32)
+
+    store.wait()
 
     @pl.loop(0, zc)
     def _(chunk):
@@ -337,35 +362,43 @@
     vmem = pl.BlockSpec(memory_space=pltpu.VMEM)
     row_sems = [pltpu.SemaphoreType.DMA((zc, rows))] * 6
     col_sems = [pltpu.SemaphoreType.DMA((cols,))] * 4
-    return pl.pallas_call(
+    far = pl.BlockSpec(memory_space=pl.ANY)
+    partial, y_terms = pl.pallas_call(
         functools.partial(section_kernel, rows, cols),
-        out_shape=jax.ShapeDtypeStruct(adjoint.shape, jnp.float32),
-        in_specs=[vmem] * 5,
-        out_specs=vmem,
+        out_shape=(
+            jax.ShapeDtypeStruct(adjoint.shape, jnp.float32),
+            jax.ShapeDtypeStruct(adjoint.shape, bf),
+        ),
+        in_specs=[far, far, vmem, vmem, vmem],
+        out_specs=(far, far),
         scratch_shapes=[
+            pltpu.VMEM((3, nz, ny, nx), jnp.float32),
+            pltpu.VMEM((3, nz, ny, nx), bf),
             pltpu.VMEM((3, nz, ny, nx), bf),
             pltpu.VMEM((3, zc, rows * ny, nx), bf),
             pltpu.VMEM((3, zc, rows * ny, nx), bf),
             pltpu.VMEM((6, ny, nz, nx), bf),
             pltpu.VMEM((6, yc, cols * nz, nx), bf),
             pltpu.VMEM((3, zc, rows * ny, nx), bf),
-            pltpu.VMEM((3, nz, ny, nx), bf),
             pltpu.VMEM((3, yc, cols * nz, nx), bf),
             pltpu.VMEM((3, ny, nz, nx), bf),
             *row_sems,
             *col_sems,
+            pltpu.SemaphoreType.DMA((zc,)),
+            pltpu.SemaphoreType.DMA((2,)),
         ],
         compiler_params=pltpu.CompilerParams(
             collective_id=0, has_side_effects=True, vmem_limit_bytes=60 * 1024 * 1024
         ),
-    )(adjoint, base_flow, stream_pair.T, normal_pair, span_pair)
+    )(adjoint, base_flow, stream_pair, normal_pair, span_pair)
+    return partial + section_step * y_terms.astype(jnp.float32)
 
 
 def section(adjoint, base_flow, stream_pair, normal_pair, span_pair):
     _, nz, ny, nx = adjoint.shape
     rows, cols = lax.axis_size("rows"), lax.axis_size("cols")
     whole = nz % 16 == 0 and ny % 16 == 0 and nx % 128 == 0
-    if whole and nz % rows == 0 and ny % cols == 0:
+    if whole and rows % 2 == 0 and nz % rows == 0 and ny % cols == 0:
         return local_kernel(adjoint, base_flow, stream_pair, normal_pair, span_pair)
     return local(adjoint, base_flow, stream_pair, normal_pair, span_pair)
 

time: 173 us -> 172 us (level); the launches traced: 170 us -> 172 us
  local copies, waits for them, and re-layouts: 6.66 us -> 0 us
  other arithmetic: 0 us -> 6.11 us
  Pallas kernels: 164 us -> 166 us
    unnamed x2 -> x0, local copies, waits for them, and re-layouts: 6.66 us -> none
    add x0 -> x1, other arithmetic: none -> 6.11 us  [local_kernel(): return partial + section_step * y_terms.astype(jnp.float32)]
    pallas_call x1, Pallas kernels: 164 us -> 166 us  [local_kernel(): pl.pallas_call(functools.partial(section_kernel, rows, cols), out_shape=(...]
where the time goes in v2:
time: 172 us
  Pallas kernels  166 us (97%)
  other arithmetic  6.11 us (4%)
    pallas_call x1, Pallas kernels, local_kernel(): pl.pallas_call(functools.partial(section_kernel, rows, cols), out_shape=(...  166 us
    add x1, other arithmetic, local_kernel(): return partial + section_step * y_terms.astype(jnp.float32)  6.11 us

profile of v2, /device:TPU:0, one launch (start us, length us, event | category | flops | bytes accessed | tf_op | source)
XLA Modules:
  0.0 171.8 jit_solution(15935960543407932968)
XLA Ops:
  0.0 165.7 %shard_map.55 = (f32[3,32,48,256]{3,2,1,0:T(8,128)}, bf16[3,32,48,256]{3,2,1,0:T(8,128)(2,1)}) custom-call(f32[3,32,48,256]{3,2,1,0:T(8,128)} %adjoint_hbm.1, bf16[3,32,48,256]{3,2,1,0:T(8,128)(2,1)} %base_hbm.1, bf16[512,256]{1,0:T(8,128)(2,1)} %stream.1, bf16[768,384]{1,0:T(8,128)(2,1)} %normal.1, bf16[256,128]{1,0:T(8,128)(2,1)} %span.1), custom_call_target="tpu_custom_call" | custom-call | tf_op jit(solution)/shard_map/pallas_call | solution.py:366
  165.7 6.1 %multiply_add_fusion = f32[3,32,48,256]{3,2,1,0:T(8,128)} fusion(f32[3,32,48,256]{3,2,1,0:T(8,128)} %get-tuple-element.7, bf16[3,32,48,256]{3,2,1,0:T(8,128)(2,1)} %get-tuple-element.8), kind=kLoop, calls=%fused_computation | loop fusion | flops 3538944 | bytes 11796480 | tf_op jit(solution)/shard_map/add | solution.py:394

commit v3 on v2

--- a/solution.py
+++ b/solution.py
@@ -99,6 +99,7 @@
     _, nz, ny, nx = out.shape
     zc = nz // rows
     yc = ny // cols
+    yp = yc // zc
     half_rows = rows // 2
     own_half = row // half_rows
 
@@ -130,9 +131,9 @@
             device_id={"rows": peer}, device_id_type=pl.DeviceIdType.MESH,
         )
 
-    def to_col(src, dst, send, recv, peer, source):
+    def to_col(src, dst, send, recv, peer, part, source):
         return pltpu.make_async_remote_copy(
-            src_ref=src, dst_ref=dst, send_sem=send.at[peer], recv_sem=recv.at[source],
+            src_ref=src, dst_ref=dst, send_sem=send.at[part, peer], recv_sem=recv.at[part, source],
             device_id={"cols": peer}, device_id_type=pl.DeviceIdType.MESH,
         )
 
@@ -165,16 +166,18 @@
             y_term.at[:, chunk, y_rows(row)], y_back.at[:, row * zc + chunk], own_sem.at[chunk]
         )
 
-    def fwd_z(peer, source):
+    def fwd_z(peer, part, source):
         return to_col(
-            z_src.at[:, pl.ds(peer * yc, yc)], z_recv.at[:, :, z_rows(source)],
-            z_send, z_recv_sem, peer, source,
-        )
-
-    def back_z(peer, source):
+            z_src.at[:, pl.ds(peer * yc + part * yp, yp)],
+            z_recv.at[:, pl.ds(part * yp, yp), z_rows(source)],
+            z_send, z_recv_sem, peer, part, source,
+        )
+
+    def back_z(peer, part, source):
         return to_col(
-            z_term.at[:, :, z_rows(peer)], z_back.at[:, pl.ds(source * yc, yc)],
-            zb_send, zb_recv, peer, source,
+            z_term.at[:, pl.ds(part * yp, yp), z_rows(peer)],
+            z_back.at[:, pl.ds(source * yc + part * yp, yp)],
+            zb_send, zb_recv, peer, part, source,
         )
 
     def row_loop(body):
@@ -199,14 +202,6 @@
         a_bf[:, z] = out[:, z].astype(jnp.bfloat16)
 
     row_loop(lambda peer: fwd_a(peer, 0, row).start())
-
-    @pl.loop(1, zc)
-    def _(chunk):
-        def both(peer):
-            fwd_a(peer, chunk, row).start()
-            fwd_u(peer, chunk, row).start()
-
-        row_loop(both)
 
     load_base.wait()
 
@@ -220,7 +215,16 @@
                 base[field, z0 : z0 + 16].astype(jnp.float32), 0, 1
             ).astype(jnp.bfloat16)
 
-    col_loop(lambda peer: fwd_z(peer, col).start())
+    @pl.loop(0, zc - 1)
+    def _(chunk):
+        def both(peer):
+            fwd_a(peer, chunk + 1, row).start()
+            fwd_u(peer, chunk + 1, row).start()
+
+        col_loop(lambda peer: fwd_z(peer, chunk, col).start())
+        row_loop(both)
+
+    col_loop(lambda peer: fwd_z(peer, zc - 1, col).start())
 
     def terms(adj, flow, own, derive, length, axis):
         half = flow[own].astype(jnp.float32)
@@ -288,33 +292,33 @@
         row_loop(lambda peer: back_y(peer, chunk, row).start())
         own_y(chunk).start()
 
-    early = zc // 2
-
-    @pl.loop(0, early)
+    def z_part(part):
+        col_loop(lambda source: fwd_z(source, part, source).wait_recv())
+
+        @pl.loop(0, yp)
+        def _(step):
+            line = part * yp + step
+            adj = [z_recv[field, line] for field in range(3)]
+            flow = [z_recv[3 + field, line] for field in range(3)]
+            for field, term in enumerate(column_terms(span, adj, flow, 2)):
+                z_term[field, line] = term.astype(jnp.bfloat16)
+
+        col_loop(lambda peer: back_z(peer, part, col).start())
+
+        @pl.loop(0, yp)
+        def _(step):
+            line = part * yp + step
+            for field in range(3):
+                z_back[field, col * yc + line] = z_term[field, line, z_rows(col), :]
+
+    @pl.loop(0, zc)
     def _(chunk):
         y_chunk(chunk)
-
-    col_loop(lambda source: fwd_z(source, source).wait_recv())
-
-    @pl.loop(0, yc)
-    def _(line):
-        adj = [z_recv[field, line] for field in range(3)]
-        flow = [z_recv[3 + field, line] for field in range(3)]
-        for field, term in enumerate(column_terms(span, adj, flow, 2)):
-            z_term[field, line] = term.astype(jnp.bfloat16)
-
-    col_loop(lambda peer: back_z(peer, col).start())
-
-    @pl.loop(0, yc)
-    def _(line):
-        for field in range(3):
-            z_back[field, col * yc + line] = z_term[field, line, z_rows(col), :]
-
-    @pl.loop(early, zc)
-    def _(chunk):
-        y_chunk(chunk)
-
-    col_loop(lambda source: back_z(source, source).wait_recv())
+        z_part(chunk)
+
+    @pl.loop(0, zc)
+    def _(part):
+        col_loop(lambda source: back_z(source, part, source).wait_recv())
 
     @pl.loop(0, 3)
     def _(field):
@@ -346,11 +350,13 @@
             fwd_u(peer, chunk, row).wait_send()
             back_y(peer, chunk, row).wait_send()
 
-    @pl.loop(1, cols)
-    def _(offset):
-        peer = col_at(offset)
-        fwd_z(peer, col).wait_send()
-        back_z(peer, col).wait_send()
+    @pl.loop(0, zc)
+    def _(part):
+        @pl.loop(1, cols)
+        def _(offset):
+            peer = col_at(offset)
+            fwd_z(peer, part, col).wait_send()
+            back_z(peer, part, col).wait_send()
 
 
 def local_kernel(adjoint, base_flow, stream_pair, normal_pair, span_pair):
@@ -361,7 +367,7 @@
     bf = jnp.bfloat16
     vmem = pl.BlockSpec(memory_space=pltpu.VMEM)
     row_sems = [pltpu.SemaphoreType.DMA((zc, rows))] * 6
-    col_sems = [pltpu.SemaphoreType.DMA((cols,))] * 4
+    col_sems = [pltpu.SemaphoreType.DMA((zc, cols))] * 4
     far = pl.BlockSpec(memory_space=pl.ANY)
     partial, y_terms = pl.pallas_call(
         functools.partial(section_kernel, rows, cols),
@@ -398,7 +404,7 @@
     _, nz, ny, nx = adjoint.shape
     rows, cols = lax.axis_size("rows"), lax.axis_size("cols")
     whole = nz % 16 == 0 and ny % 16 == 0 and nx % 128 == 0
-    if whole and rows % 2 == 0 and nz % rows == 0 and ny % cols == 0:
+    if whole and rows % 2 == 0 and nz % rows == 0 and ny % (cols * (nz // rows)) == 0:
         return local_kernel(adjoint, base_flow, stream_pair, normal_pair, span_pair)
     return local(adjoint, base_flow, stream_pair, normal_pair, span_pair)
 

time: 172 us -> 173 us (level)
  no operation moved by 1% of the time
where the time goes in v3:
time: 173 us; the launch traced here: 172 us
  Pallas kernels  166 us (96%)
  other arithmetic  6.11 us (4%)
    pallas_call x1, Pallas kernels, local_kernel(): pl.pallas_call(functools.partial(section_kernel, rows, cols), out_shape=(...  166 us
    add x1, other arithmetic, local_kernel(): return partial + section_step * y_terms.astype(jnp.float32)  6.11 us

profile of v3, /device:TPU:0, one launch (start us, length us, event | category | flops | bytes accessed | tf_op | source)
XLA Modules:
  0.0 172.4 jit_solution(6339139090009439767)
XLA Ops:
  0.0 166.2 %shard_map.55 = (f32[3,32,48,256]{3,2,1,0:T(8,128)}, bf16[3,32,48,256]{3,2,1,0:T(8,128)(2,1)}) custom-call(f32[3,32,48,256]{3,2,1,0:T(8,128)} %adjoint_hbm.1, bf16[3,32,48,256]{3,2,1,0:T(8,128)(2,1)} %base_hbm.1, bf16[512,256]{1,0:T(8,128)(2,1)} %stream.1, bf16[768,384]{1,0:T(8,128)(2,1)} %normal.1, bf16[256,128]{1,0:T(8,128)(2,1)} %span.1), custom_call_target="tpu_custom_call" | custom-call | tf_op jit(solution)/shard_map/pallas_call | solution.py:372
  166.3 6.1 %multiply_add_fusion = f32[3,32,48,256]{3,2,1,0:T(8,128)} fusion(f32[3,32,48,256]{3,2,1,0:T(8,128)} %get-tuple-element.7, bf16[3,32,48,256]{3,2,1,0:T(8,128)(2,1)} %get-tuple-element.8), kind=kLoop, calls=%fused_computation | loop fusion | flops 3538944 | bytes 11796480 | tf_op jit(solution)/shard_map/add | solution.py:400

commit v4 on v3

--- a/solution.py
+++ b/solution.py
@@ -215,16 +215,19 @@
                 base[field, z0 : z0 + 16].astype(jnp.float32), 0, 1
             ).astype(jnp.bfloat16)
 
-    @pl.loop(0, zc - 1)
-    def _(chunk):
+    def send_y(chunk):
         def both(peer):
-            fwd_a(peer, chunk + 1, row).start()
-            fwd_u(peer, chunk + 1, row).start()
-
-        col_loop(lambda peer: fwd_z(peer, chunk, col).start())
+            fwd_a(peer, chunk, row).start()
+            fwd_u(peer, chunk, row).start()
+
         row_loop(both)
 
-    col_loop(lambda peer: fwd_z(peer, zc - 1, col).start())
+    if zc > 1:
+        send_y(1)
+
+    @pl.loop(0, zc)
+    def _(part):
+        col_loop(lambda peer: fwd_z(peer, part, col).start())
 
     def terms(adj, flow, own, derive, length, axis):
         half = flow[own].astype(jnp.float32)
@@ -283,6 +286,10 @@
             source = row_at(offset)
             fwd_a(source, chunk, source).wait_recv()
             fwd_u(source, chunk, source).wait_recv()
+
+        @pl.when(chunk + 2 < zc)
+        def _():
+            send_y(chunk + 2)
 
         adj = [y_a[field, chunk] for field in range(3)]
         flow = [y_u[field, chunk] for field in range(3)]

time: 173 us -> 173 us (level)
  no operation moved by 1% of the time
where the time goes in v4:
time: 173 us; the launch traced here: 172 us
  Pallas kernels  166 us (96%)
  other arithmetic  6.11 us (4%)
    pallas_call x1, Pallas kernels, local_kernel(): pl.pallas_call(functools.partial(section_kernel, rows, cols), out_shape=(...  166 us
    add x1, other arithmetic, local_kernel(): return partial + section_step * y_terms.astype(jnp.float32)  6.11 us

profile of v4, /device:TPU:0, one launch (start us, length us, event | category | flops | bytes accessed | tf_op | source)
XLA Modules:
  0.0 172.4 jit_solution(17165350303367393530)
XLA Ops:
  0.0 166.3 %shard_map.55 = (f32[3,32,48,256]{3,2,1,0:T(8,128)}, bf16[3,32,48,256]{3,2,1,0:T(8,128)(2,1)}) custom-call(f32[3,32,48,256]{3,2,1,0:T(8,128)} %adjoint_hbm.1, bf16[3,32,48,256]{3,2,1,0:T(8,128)(2,1)} %base_hbm.1, bf16[512,256]{1,0:T(8,128)(2,1)} %stream.1, bf16[768,384]{1,0:T(8,128)(2,1)} %normal.1, bf16[256,128]{1,0:T(8,128)(2,1)} %span.1), custom_call_target="tpu_custom_call" | custom-call | tf_op jit(solution)/shard_map/pallas_call | solution.py:379
  166.3 6.1 %multiply_add_fusion = f32[3,32,48,256]{3,2,1,0:T(8,128)} fusion(f32[3,32,48,256]{3,2,1,0:T(8,128)} %get-tuple-element.7, bf16[3,32,48,256]{3,2,1,0:T(8,128)(2,1)} %get-tuple-element.8), kind=kLoop, calls=%fused_computation | loop fusion | flops 3538944 | bytes 11796480 | tf_op jit(solution)/shard_map/add | solution.py:407
